TPU v7x, 32 devices: a whole 2x2x4 slice. The times are simulated.
32 devices in a mesh: dp: 8 (over z, x), feat: 4 (over y, core).
Axes of the slice: x: 2, y: 2, z: 4, core: 2. Of those that a mesh axis runs over, the one named last changes fastest.
Arguments:
- samples: bfloat16 [8192, 1024], P('dp', 'feat'), may hold values from -6 to 6
- freqs: bfloat16 [1024, 32768], P('dp', 'feat'), may hold values from -0.1875 to 0.1875
- phases: float32 [32768], P('feat'), may hold values from -3.140625 to 3.140625
- range_test: bfloat16 [32768, 256], P('feat'), may hold values from -6 to 6
- corange_test: bfloat16 [256, 8192], P(None, 'dp'), may hold values from -6 to 6
Outputs:
- range_sketch: float32 [8192, 256], P(('dp', 'feat'))
- corange_sketch: float32 [256, 32768], P('dp', 'feat')
All inputs are finite; a program needn't handle non-finite values.
Results may differ from a plain program's by a relative error of at most 0.0024.
Values may be sent and summed in bfloat16 or wider, within the bound.
A program may use at most 128 MiB of HBM per device.

v0:
```python
import math
import jax
import jax.numpy as jnp
from jax import lax
from jax.sharding import PartitionSpec as P


def on_device(samples, freqs, phases, range_test, corange_test):
    gathered = lax.all_gather(samples, "feat", axis=1, tiled=True)
    feature_count = freqs.shape[1]
    projection = jnp.dot(
        gathered,
        lax.all_gather(freqs, "dp", axis=0, tiled=True),
        preferred_element_type=jnp.float32,
    )
    scale = math.sqrt(2.0 / (feature_count * lax.axis_size("feat")))
    features = (scale * jnp.cos(projection + phases[None, :])).astype(jnp.bfloat16)
    range_sketch = lax.psum_scatter(
        jnp.dot(features, range_test, preferred_element_type=jnp.float32),
        "feat",
        scatter_dimension=0,
        tiled=True,
    )
    corange_sketch = lax.psum_scatter(
        jnp.dot(corange_test, features, preferred_element_type=jnp.float32),
        "dp",
        scatter_dimension=0,
        tiled=True,
    )
    return (range_sketch, corange_sketch)


def solution(mesh):
    placed = (P("dp", "feat"), P("dp", "feat"), P("feat"), P("feat", None), P(None, "dp"))
    return jax.shard_map(
        on_device,
        mesh=mesh,
        in_specs=placed,
        out_specs=(P(("dp", "feat"), None), P("dp", "feat")),
        check_vma=False,
    )
```

profile of v0, /device:TPU:0, one launch (start us, length us, event | category | flops | bytes accessed | tf_op | source)
XLA Modules:
  0.0 583.5 jit_solution(11586309907684146967)
XLA Ops:
  7.2 0.0 copy-start
  7.2 0.0 all-gather.3.cloned.1.call-start
  7.2 0.7 all-gather.3.cloned.1.call-update
  7.9 0.0 all-gather.5.cloned.1.call-start
  8.0 0.7 all-gather.5.cloned.1.call-update
  8.7 0.0 reduce-scatter.5.cloned.1.call-start
  8.7 26.4 %all-gather.3.cloned.1.call-done = bf16[1024,1024]{1,0:T(8,128)(2,1)} async-done(((bf16[1024,256]{1,0:T(8,128)(2,1)}), bf16[1024,1024]{1,0:T(8,128)(2,1)}) %all-gather.3.cloned.1.call-update) | async-done | bytes 2097168 | tf_op jit(solution)/shard_map/all_gather | solution.py:9
  35.1 229.8 %all-gather.5.cloned.1.call-done = bf16[1024,8192]{1,0:T(8,128)(2,1)} async-done(((bf16[128,8192]{1,0:T(8,128)(2,1)}), bf16[1024,8192]{1,0:T(8,128)(2,1)}) %all-gather.5.cloned.1.call-update) | async-done | bytes 16777232 | tf_op jit(solution)/shard_map/all_gather | solution.py:13
  264.9 0.0 copy-start.1
  264.9 124.0 %multiply_convert_fusion = bf16[1024,8192]{1,0:T(8,128)(2,1)S(1)} fusion(bf16[1024,1024]{1,0:T(8,128)(2,1)} %all-gather.3.cloned.1.call-done, bf16[1024,8192]{1,0:T(8,128)(2,1)} %all-gather.5.cloned.1.call-done, f32[8192]{0:T(1024)} %param.7), kind=kOutput, calls=%fused_computation | convolution fusion | flops 17205035008 | bytes 35684352 | tf_op jit(solution)/shard_map/dot_general | solution.py:11
  388.9 0.0 copy-start.2
  388.9 5.7 copy-done.2
  394.6 0.0 copy-done.1
  394.6 5.5 fusion
  400.2 0.0 reduce-scatter.5.cloned.1.call-update
  400.2 0.0 reduce-scatter.7.cloned.1.call-start
  400.2 0.0 copy-done
  400.3 14.1 %convolution_bitcast_fusion = f32[256,8192]{0,1:T(8,128)} fusion(bf16[1024,8192]{1,0:T(8,128)(2,1)} %copy-done.2, bf16[256,1024]{1,0:T(8,128)(2,1)S(1)} %copy-done), kind=kOutput, calls=%fused_computation.1 | convolution fusion | flops 4294967296 | bytes 25690112 | tf_op jit(solution)/shard_map/dot_general | solution.py:25
  414.3 9.0 %copy.9 = f32[256,8192]{1,0:T(8,128)} copy(f32[256,8192]{0,1:T(8,128)} %convolution_bitcast_fusion) | data formatting | bytes 16777216
  423.3 0.0 reduce-scatter.7.cloned.1.call-update
  423.3 0.1 reduce-scatter.5.cloned.1.call-done
  423.4 153.5 %reduce-scatter.7.cloned.1.call-done = f32[32,8192]{1,0:T(8,128)} async-done(((f32[256,8192]{1,0:T(8,128)}), f32[32,8192]{1,0:T(8,128)}) %reduce-scatter.7.cloned.1.call-update) | async-done | bytes 1048592
Async XLA Ops:
  7.2 393.1 %copy-start = (bf16[256,1024]{1,0:T(8,128)(2,1)S(1)}, bf16[256,1024]{1,0:T(8,128)(2,1)}, u32[]{:S(2)}) copy-start(bf16[256,1024]{1,0:T(8,128)(2,1)} %param.9) | copy-start | bytes 1572868
  7.2 28.0 %all-gather.3.cloned.1.call-start = ((), (), s32[]{:S(2)}) async-start(), calls=%async_computation.2 | async-start | bytes 2621440 | tf_op jit(solution)/shard_map/all_gather | solution.py:9
  7.9 257.0 %all-gather.5.cloned.1.call-start = ((), (), s32[]{:S(2)}) async-start(), calls=%async_computation.3 | async-start | bytes 18874368 | tf_op jit(solution)/shard_map/all_gather | solution.py:13
  8.7 414.8 %reduce-scatter.5.cloned.1.call-start = ((), (), s32[]{:S(2)}) async-start(), calls=%async_computation.4 | async-start | bytes 1310720 | tf_op jit(solution)/shard_map/reduce_scatter | solution.py:18
  264.9 129.7 %copy-start.1 = (bf16[8192,256]{1,0:T(8,128)(2,1)S(1)}, bf16[8192,256]{1,0:T(8,128)(2,1)}, u32[]{:S(2)}) copy-start(bf16[8192,256]{1,0:T(8,128)(2,1)} %param.8) | copy-start | bytes 12582916
  388.9 5.7 copy-start.2
  400.2 176.8 %reduce-scatter.7.cloned.1.call-start = ((), (), s32[]{:S(2)}) async-start(), calls=%async_computation.5 | async-start | bytes 9437184
Sparse Core Ops, SparseCore 0:
  9.6 25.5 all-gather.2
  37.3 227.5 all-gather.4
  400.3 23.0 reduce-scatter.4
  427.9 149.0 reduce-scatter.6
where the time goes:
time: 584 us
  waiting for transfers between devices  411 us (70%)
  matrix products  144 us (25%)
  local copies, waits for them, and re-layouts  14.7 us (3%)
  between operations  13.8 us (2%)
    all_gather x1, waiting for transfers between devices, on_device(): lax.all_gather(freqs, 'dp', axis=0, tiled=True)  230 us
    unnamed x5, waiting for transfers between devices  155 us
    dot_general x1, matrix products, on_device(): jnp.dot(gathered, lax.all_gather(freqs, 'dp', axis=0, tiled=True), prefer...  124 us
    all_gather x1, waiting for transfers between devices, on_device(): gathered = lax.all_gather(samples, 'feat', axis=1, tiled=True)  26.4 us
    unnamed x7, local copies, waits for them, and re-layouts  14.7 us
    dot_general x1, matrix products, on_device(): jnp.dot(corange_test, features, preferred_element_type=jnp.float32)  14.1 us
  transfers between devices with their start and end apart: 4, of which 4 were waited for; matrix products, arithmetic and copies ran while one was open for 4% of the time, Pallas kernels for 0%

commit v1 on v0

--- a/solution.py
+++ b/solution.py
@@ -6,7 +6,16 @@
 
 
 def on_device(samples, freqs, phases, range_test, corange_test):
-    gathered = lax.all_gather(samples, "feat", axis=1, tiled=True)
+    devices, position, rows = (lax.axis_size("feat"), lax.axis_index("feat"), samples.shape[1])
+    right = [(i, (i + 1) % devices) for i in range(devices)]
+    out = jnp.zeros((*samples.shape[:1], devices * rows, *samples.shape[1 + 1 :]), samples.dtype)
+    carried = samples
+    for turn in range(devices):
+        owner = (position - turn) % devices
+        out = lax.dynamic_update_slice_in_dim(out, carried, owner * rows, axis=1)
+        if turn < devices - 1:
+            carried = lax.ppermute(carried, "feat", right)
+    gathered = out
     feature_count = freqs.shape[1]
     projection = jnp.dot(
         gathered,

time: 584 us -> 561 us (0.961)
  waiting for transfers between devices: 411 us -> 383 us
    all_gather x1 -> x0, waiting for transfers between devices: 26.4 us -> none  [on_device(): gathered = lax.all_gather(samples, 'feat', axis=1, tiled=True)]
    all_gather x1, waiting for transfers between devices: 230 us -> 204 us  [on_device(): lax.all_gather(freqs, 'dp', axis=0, tiled=True)]
    ppermute x0 -> x3, waiting for transfers between devices: none -> 24.1 us  [on_device(): carried = lax.ppermute(carried, 'feat', right)]
    unnamed x5 -> x4, waiting for transfers between devices: 155 us -> 154 us
    unnamed x7 -> x9, local copies, waits for them, and re-layouts: 14.7 us -> 14.7 us
  transfers between devices with their start and end apart: 4 -> 6, of which waited for: 4 -> 5; matrix products, arithmetic and copies ran while one was open for 4% -> 5% of each run, Pallas kernels for 0% -> 0%
where the time goes in v1:
time: 561 us
  waiting for transfers between devices  383 us (68%)
  matrix products  145 us (26%)
  local copies, waits for them, and re-layouts  18.3 us (3%)
  between operations  13.8 us (2%)
    all_gather x1, waiting for transfers between devices, on_device(): lax.all_gather(freqs, 'dp', axis=0, tiled=True)  204 us
    unnamed x4, waiting for transfers between devices  154 us
    dot_general x1, matrix products, on_device(): jnp.dot(gathered, lax.all_gather(freqs, 'dp', axis=0, tiled=True), prefer...  125 us
    ppermute x3, waiting for transfers between devices, on_device(): carried = lax.ppermute(carried, 'feat', right)  24.1 us
    unnamed x9, local copies, waits for them, and re-layouts  14.7 us
    dot_general x1, matrix products, on_device(): jnp.dot(corange_test, features, preferred_element_type=jnp.float32)  14.1 us
  transfers between devices with their start and end apart: 6, of which 5 were waited for; matrix products, arithmetic and copies ran while one was open for 5% of the time, Pallas kernels for 0%

profile of v1, /device:TPU:0, one launch (start us, length us, event | category | flops | bytes accessed | tf_op | source)
XLA Modules:
  0.0 560.6 jit_solution(11598233955838648018)
XLA Ops:
  7.2 0.0 copy-start
  7.2 0.0 copy-start.2
  7.2 0.0 all-gather.2.cloned.1.call-start
  7.2 0.7 all-gather.2.cloned.1.call-update
  7.9 0.0 reduce-scatter.5.cloned.1.call-start
  8.0 0.5 collective-permute-start
  8.5 9.0 %collective-permute-done = bf16[1024,256]{1,0:T(8,128)(2,1)S(1)} collective-permute-done((bf16[1024,256]{1,0:T(8,128)(2,1)}, bf16[1024,256]{1,0:T(8,128)(2,1)S(1)}, u32[]{:S(2)}, u32[]{:S(2)}) %collective-permute-start) | collective-permute-done | bytes 524320 | tf_op jit(solution)/shard_map/ppermute | solution.py:17
  17.5 0.0 collective-permute-start.1
  17.5 8.7 %collective-permute-done.1 = bf16[1024,256]{1,0:T(8,128)(2,1)} collective-permute-done((bf16[1024,256]{1,0:T(8,128)(2,1)S(1)}, bf16[1024,256]{1,0:T(8,128)(2,1)}, u32[]{:S(2)}, u32[]{:S(2)}) %collective-permute-start.1) | collective-permute-done | bytes 524320 | tf_op jit(solution)/shard_map/ppermute | solution.py:17
  26.2 0.0 collective-permute-start.2
  26.2 0.3 broadcast_in_dim.4
  26.5 1.1 constant_dynamic-update-slice_fusion.3
  27.6 0.1 constant_dynamic-update-slice_fusion.2
  27.7 1.1 constant_dynamic-update-slice_fusion.1
  28.8 6.4 %collective-permute-done.2 = bf16[1024,256]{1,0:T(8,128)(2,1)} collective-permute-done((bf16[1024,256]{1,0:T(8,128)(2,1)}, bf16[1024,256]{1,0:T(8,128)(2,1)}, u32[]{:S(2)}, u32[]{:S(2)}) %collective-permute-start.2) | collective-permute-done | bytes 524320 | tf_op jit(solution)/shard_map/ppermute | solution.py:17
  35.1 1.1 constant_dynamic-update-slice_fusion
  36.2 204.2 %all-gather.2.cloned.1.call-done = bf16[1024,8192]{1,0:T(8,128)(2,1)} async-done(((bf16[128,8192]{1,0:T(8,128)(2,1)}), bf16[1024,8192]{1,0:T(8,128)(2,1)}) %all-gather.2.cloned.1.call-update) | async-done | bytes 16777232 | tf_op jit(solution)/shard_map/all_gather | solution.py:22
  240.5 0.0 copy-done.2
  240.5 0.0 copy-start.1
  240.5 125.4 %multiply_convert_fusion = bf16[1024,8192]{1,0:T(8,128)(2,1)S(1)} fusion(bf16[1024,1024]{1,0:T(8,128)(2,1)S(1)} %constant_dynamic-update-slice_fusion, bf16[1024,8192]{1,0:T(8,128)(2,1)} %all-gather.2.cloned.1.call-done, f32[8192]{0:T(1024)S(1)} %copy-done.2), kind=kOutput, calls=%fused_computation | convolution fusion | flops 17205035008 | bytes 35684352 | tf_op jit(solution)/shard_map/dot_general | solution.py:20
  365.9 0.0 copy-start.3
  365.9 5.7 %copy-done.3 = bf16[1024,8192]{1,0:T(8,128)(2,1)} copy-done((bf16[1024,8192]{1,0:T(8,128)(2,1)}, bf16[1024,8192]{1,0:T(8,128)(2,1)S(1)}, u32[]{:S(2)}) %copy-start.3) | copy-done | bytes 16777240
  371.6 0.0 copy-done.1
  371.6 5.6 fusion
  377.2 0.0 reduce-scatter.5.cloned.1.call-update
  377.2 0.2 reduce-scatter.7.cloned.1.call-start
  377.4 0.0 copy-done
  377.5 14.1 %convolution_bitcast_fusion = f32[256,8192]{0,1:T(8,128)} fusion(bf16[1024,8192]{1,0:T(8,128)(2,1)} %copy-done.3, bf16[256,1024]{1,0:T(8,128)(2,1)S(1)} %copy-done), kind=kOutput, calls=%fused_computation.1 | convolution fusion | flops 4294967296 | bytes 25690112 | tf_op jit(solution)/shard_map/dot_general | solution.py:34
  391.6 8.9 %copy.9 = f32[256,8192]{1,0:T(8,128)} copy(f32[256,8192]{0,1:T(8,128)} %convolution_bitcast_fusion) | data formatting | bytes 16777216
  400.5 0.0 reduce-scatter.7.cloned.1.call-update
  400.5 0.0 reduce-scatter.5.cloned.1.call-done
  400.6 153.5 %reduce-scatter.7.cloned.1.call-done = f32[32,8192]{1,0:T(8,128)} async-done(((f32[256,8192]{1,0:T(8,128)}), f32[32,8192]{1,0:T(8,128)}) %reduce-scatter.7.cloned.1.call-update) | async-done | bytes 1048592
Async XLA Ops:
  7.2 370.3 %copy-start = (bf16[256,1024]{1,0:T(8,128)(2,1)S(1)}, bf16[256,1024]{1,0:T(8,128)(2,1)}, u32[]{:S(2)}) copy-start(bf16[256,1024]{1,0:T(8,128)(2,1)} %param.9) | copy-start | bytes 1572868
  7.2 233.3 %copy-start.2 = (f32[8192]{0:T(1024)S(1)}, f32[8192]{0:T(1024)}, u32[]{:S(2)}) copy-start(f32[8192]{0:T(1024)} %param.7) | copy-start | bytes 98308
  7.2 233.3 %all-gather.2.cloned.1.call-start = ((), (), s32[]{:S(2)}) async-start(), calls=%async_computation.2 | async-start | bytes 18874368 | tf_op jit(solution)/shard_map/all_gather | solution.py:22
  7.9 392.6 %reduce-scatter.5.cloned.1.call-start = ((), (), s32[]{:S(2)}) async-start(), calls=%async_computation.3 | async-start | bytes 1310720 | tf_op jit(solution)/shard_map/reduce_scatter | solution.py:27
  8.0 9.5 %collective-permute-start = (bf16[1024,256]{1,0:T(8,128)(2,1)}, bf16[1024,256]{1,0:T(8,128)(2,1)S(1)}, u32[]{:S(2)}, u32[]{:S(2)}) collective-permute-start(bf16[1024,256]{1,0:T(8,128)(2,1)} %param.5), channel_id=1, source_target_pairs={{0,1},{1,2},{2,3},{3,0},{4,5},{5,6},{6,7},{7,4},{8,9},{9,10},{10,1... | collective-permute-start | bytes 1572872 | tf_op jit(solution)/shard_map/ppermute | solution.py:17
  17.5 8.7 %collective-permute-start.1 = (bf16[1024,256]{1,0:T(8,128)(2,1)S(1)}, bf16[1024,256]{1,0:T(8,128)(2,1)}, u32[]{:S(2)}, u32[]{:S(2)}) collective-permute-start(bf16[1024,256]{1,0:T(8,128)(2,1)S(1)} %collective-permute-done), channel_id=1, source_target_pairs={{0,1},{1,2},{2,3},{3,0},{4,5},{5,6},{6,7},{7,4},{8,9},{9,10},{10,1... | collective-permute-start | bytes 1572872 | tf_op jit(solution)/shard_map/ppermute | solution.py:17
  26.2 8.9 %collective-permute-start.2 = (bf16[1024,256]{1,0:T(8,128)(2,1)}, bf16[1024,256]{1,0:T(8,128)(2,1)}, u32[]{:S(2)}, u32[]{:S(2)}) collective-permute-start(bf16[1024,256]{1,0:T(8,128)(2,1)} %collective-permute-done.1), channel_id=1, source_target_pairs={{0,1},{1,2},{2,3},{3,0},{4,5},{5,6},{6,7},{7,4},{8,9},{9,10},{10,1... | collective-permute-start | bytes 1572872 | tf_op jit(solution)/shard_map/ppermute | solution.py:17
  240.5 131.2 %copy-start.1 = (bf16[8192,256]{1,0:T(8,128)(2,1)S(1)}, bf16[8192,256]{1,0:T(8,128)(2,1)}, u32[]{:S(2)}) copy-start(bf16[8192,256]{1,0:T(8,128)(2,1)} %param.8) | copy-start | bytes 12582916
  365.9 5.7 %copy-start.3 = (bf16[1024,8192]{1,0:T(8,128)(2,1)}, bf16[1024,8192]{1,0:T(8,128)(2,1)S(1)}, u32[]{:S(2)}) copy-start(bf16[1024,8192]{1,0:T(8,128)(2,1)S(1)} %multiply_convert_fusion) | copy-start | bytes 50331652
  377.2 176.9 %reduce-scatter.7.cloned.1.call-start = ((), (), s32[]{:S(2)}) async-start(), calls=%async_computation.4 | async-start | bytes 9437184
Sparse Core Ops, SparseCore 0:
  10.1 230.2 all-gather.1
  377.3 23.0 reduce-scatter.4
  405.1 148.9 reduce-scatter.6
